TPU v7x, 32 devices: a whole 2x2x4 slice. The times are simulated.
32 devices in a mesh: replica: 2 (over x), side: 4 (over y, core), tp: 4 (over z).
Axes of the slice: x: 2, y: 2, z: 4, core: 2. Of those that a mesh axis runs over, the one named last changes fastest.
Arguments:
- queries: bfloat16 [4096, 4096], P(('replica', 'side'), 'tp'), parts along dimension 0, may hold values from -60 to 60
- new_keys: bfloat16 [4096, 512], P(('replica', 'side')), parts along dimension 0, may hold values from -6 to 6
- new_values: bfloat16 [4096, 512], P(('replica', 'side')), parts along dimension 0, may hold values from -6 to 6
- cache_keys: bfloat16 [8, 512, 512], P(('replica', 'side'), 'tp'), parts along dimension 0, may hold values from -6 to 6
- cache_values: bfloat16 [8, 512, 512], P(('replica', 'side'), 'tp'), parts along dimension 0, may hold values from -6 to 6
- out_weight: bfloat16 [4096, 2048], P('tp'), may hold values from -0.09375 to 0.09375
- residual: bfloat16 [4096, 2048], P(('replica', 'side', 'tp')), parts along dimension 0, may hold values from -40 to 40
- norm_gain: bfloat16 [2048], replicated, may hold values from 0.099609375 to 1.8984375
- gate_weight: bfloat16 [16, 2048, 768], P(('side', 'tp')), may hold values from -0.125 to 0.125
- up_weight: bfloat16 [16, 2048, 768], P(('side', 'tp')), may hold values from -0.125 to 0.125
- down_weight: bfloat16 [16, 768, 2048], P(('side', 'tp')), may hold values from -0.21875 to 0.21875
- expert_ids: int32 [4096, 8], P(('replica', 'side', 'tp')), parts along dimension 0, may hold values from 0 to 15, all different within a row; in each aligned block of 128 rows (0 to 127, 128 to 255, ...) at most 128 rows name the same one
- numerators: int32 [4096, 8], P(('replica', 'side', 'tp')), parts along dimension 0, may hold values from 1 to 32767
Outputs:
- output: float32 [4096, 2048], P(('replica', 'side', 'tp')), parts along dimension 0
There are 2 independent parts, one for each index of `replica`. A program takes and returns all parts, laid end to end along the dimension named above; an argument that names none is the same for every part. Nothing has to cross between parts.
Inputs may be any that keep to these rules, and one draw needn't show every extreme that they name: `expert_ids`: each row names 8 different experts. Among the rows of one device (aligned blocks of 128 rows) no expert is named by more than 128 rows, and in every draw some expert is named by exactly 128 rows of some device.
All inputs are finite; a program needn't handle non-finite values.
Results may differ from a plain program's by a relative error of at most 0.0035.
Values may be sent and summed in bfloat16 or wider, within the bound.
A program may use at most 128 MiB of HBM per device.

v0:
```python
import math

import jax
import jax.numpy as jnp
from jax import lax
from jax.sharding import PartitionSpec as P

D = 2048
H = 32
KV = 4
HD = 128


def pick_heads(block_rows, head_kv):
    length_now = block_rows.shape[0]
    shaped = block_rows.reshape(length_now, KV, HD)
    return jnp.take(shaped, head_kv, axis=1)


def softmax_update(state_now, scores, values):
    running, totals, context = state_now
    highest = jnp.maximum(running, jnp.max(scores, axis=-1))
    factor = jnp.exp(running - highest)
    exponent = jnp.exp(scores - highest[..., None])
    totals = totals * factor + jnp.sum(exponent, axis=-1)
    context = context * factor[..., None] + jnp.einsum(
        "hrn,nhd->hrd", exponent.astype(jnp.bfloat16), values, preferred_element_type=jnp.float32
    )
    return (highest, totals, context)


def local(
    queries,
    new_keys,
    new_values,
    cache_keys,
    cache_values,
    out_weight,
    residual,
    norm_gain,
    gate_weight,
    up_weight,
    down_weight,
    expert_ids,
    numerators,
):
    tp_count = lax.axis_size("tp")
    side_count = lax.axis_size("side")
    group_rows = queries.shape[0]
    local_heads = queries.shape[1] // HD
    head_kv = (lax.axis_index("tp") * local_heads + jnp.arange(local_heads)) // (H // KV)
    query_heads = queries.reshape(group_rows, local_heads, HD)
    score_scale = 1.0 / math.sqrt(HD)
    initial = (
        jnp.full((local_heads, group_rows), -1e30, jnp.float32),
        jnp.zeros((local_heads, group_rows), jnp.float32),
        jnp.zeros((local_heads, group_rows, HD), jnp.float32),
    )
    key_piece = pick_heads(lax.all_gather(cache_keys, "tp", axis=1, tiled=True)[0], head_kv)
    value_piece = pick_heads(lax.all_gather(cache_values, "tp", axis=1, tiled=True)[0], head_kv)
    scores = (
        jnp.einsum("rhd,nhd->hrn", query_heads, key_piece, preferred_element_type=jnp.float32)
        * score_scale
    )
    state_now = softmax_update(initial, scores, value_piece)
    own_keys = pick_heads(new_keys, head_kv)
    own_values = pick_heads(new_values, head_kv)
    scores = (
        jnp.einsum("rhd,nhd->hrn", query_heads, own_keys, preferred_element_type=jnp.float32)
        * score_scale
    )
    positions = jnp.arange(group_rows)
    visible = positions[None, :] <= positions[:, None]
    scores = jnp.where(visible[None], scores, -1e30)
    running, totals, context = softmax_update(state_now, scores, own_values)
    attended = (
        (context / totals[..., None])
        .transpose(1, 0, 2)
        .reshape(group_rows, local_heads * HD)
        .astype(jnp.bfloat16)
    )
    own_rows = residual.shape[0]
    attn_out = lax.psum_scatter(
        jnp.dot(attended, out_weight, preferred_element_type=jnp.float32).astype(jnp.bfloat16),
        "tp",
        scatter_dimension=0,
        tiled=True,
    ).astype(jnp.float32)
    stream = residual.astype(jnp.float32) + attn_out
    normed = (
        stream
        * lax.rsqrt(jnp.mean(stream * stream, axis=-1, keepdims=True) + 1e-06)
        * norm_gain.astype(jnp.float32)
    ).astype(jnp.bfloat16)
    experts_all = side_count * tp_count
    top_count = expert_ids.shape[1]
    copies = own_rows * top_count
    capacity = max(2, 2 * copies // experts_all)
    flat_ids = expert_ids.reshape(copies)
    one_hot = (flat_ids[:, None] == jnp.arange(experts_all)[None, :]).astype(jnp.int32)
    earlier = jnp.cumsum(one_hot, axis=0) - one_hot
    slot_rank = jnp.sum(earlier * one_hot, axis=1)
    slot_index = flat_ids * capacity + slot_rank
    owners = jnp.arange(copies) // top_count
    outgoing = (
        jnp.zeros((experts_all * capacity, D), jnp.bfloat16).at[slot_index].set(normed[owners])
    )
    outgoing = outgoing.reshape(experts_all, capacity, D)
    buffer = lax.all_to_all(outgoing, ("side", "tp"), split_axis=0, concat_axis=0, tiled=True)
    buffer_shape = buffer.shape
    flat_rows = buffer.reshape(-1, D)
    gate_sum = jnp.dot(flat_rows, gate_weight[0], preferred_element_type=jnp.float32)
    upward = jnp.dot(flat_rows, up_weight[0], preferred_element_type=jnp.float32)
    hidden = (jax.nn.silu(gate_sum) * upward).astype(jnp.bfloat16)
    returned = lax.all_to_all(
        jnp.dot(hidden, down_weight[0], preferred_element_type=jnp.float32)
        .astype(jnp.bfloat16)
        .reshape(buffer_shape),
        ("side", "tp"),
        split_axis=0,
        concat_axis=0,
        tiled=True,
    )
    gathered = returned.reshape(experts_all * capacity, D)[slot_index]
    weights = numerators.astype(jnp.float32)
    weights = weights / jnp.sum(weights, axis=1, keepdims=True)
    mixture = jnp.sum(
        weights[:, :, None] * gathered.reshape(own_rows, top_count, D).astype(jnp.float32), axis=1
    )
    return stream + mixture


def solution(mesh):
    in_specs = (
        P(("replica", "side"), "tp"),
        P(("replica", "side"), None),
        P(("replica", "side"), None),
        P(("replica", "side"), "tp", None),
        P(("replica", "side"), "tp", None),
        P("tp", None),
        P(("replica", "side", "tp"), None),
        P(),
        P(("side", "tp"), None, None),
        P(("side", "tp"), None, None),
        P(("side", "tp"), None, None),
        P(("replica", "side", "tp"), None),
        P(("replica", "side", "tp"), None),
    )
    out_specs = P(("replica", "side", "tp"), None)
    return jax.shard_map(local, mesh=mesh, in_specs=in_specs, out_specs=out_specs, check_vma=False)
```

profile of v0, /device:TPU:0, one launch (start us, length us, event | category | flops | bytes accessed | tf_op | source)
XLA Modules:
  0.0 598.7 jit_solution(12248745915956067718)
XLA Ops:
  6.6 0.1 iota_compare_fusion
  6.7 2.2 copy.40
  8.9 2.1 copy.41
  10.9 1.0 copy.33
  12.0 17.1 %all_gather.6 = bf16[1,512,512]{1,2,0:T(8,128)(2,1)} all-gather(bf16[1,128,512]{1,2,0:T(8,128)(2,1)S(1)} %copy.33), channel_id=1, replica_groups=mesh['replica'=2,'side'=4,'tp'=4] {'tp'}, dimensions={1}, use_global_device_ids=true | all-gather | bytes 655360 | tf_op jit(solution)/shard_map/all_gather | solution.py:59
  29.0 2.1 copy.34
  31.1 2.7 gather_fusion.3
  33.8 2.7 gather_fusion.1
  36.5 1.0 copy.36
  37.5 15.4 %all_gather.7 = bf16[1,512,512]{1,2,0:T(8,128)(2,1)} all-gather(bf16[1,128,512]{1,2,0:T(8,128)(2,1)S(1)} %copy.36), channel_id=1, replica_groups=mesh['replica'=2,'side'=4,'tp'=4] {'tp'}, dimensions={1}, use_global_device_ids=true | all-gather | bytes 655360 | tf_op jit(solution)/shard_map/all_gather | solution.py:60
  52.9 2.0 copy.37
  55.0 2.8 gather_fusion.2
  57.7 2.1 copy.43
  59.8 2.0 copy.44
  61.8 2.7 gather_fusion.4
  64.5 3.0 bitcast_reduce_fusion
  67.6 1.8 fusion.6
  69.4 3.1 fusion.7
  72.5 3.7 fusion.2
  76.2 0.0 copy-start.9
  76.2 4.6 fusion.27
  80.8 0.0 copy-start.6
  80.9 3.8 convolution_convert_fusion.1
  84.7 0.0 reduce-scatter.2.cloned.1.call-update
  84.7 0.1 copy.49
  84.8 0.1 eq.29
  84.9 0.1 eq.25
  85.0 4.5 reduce-window.6
  89.5 0.1 slice.20
  89.6 0.1 copy.51
  89.8 0.1 copy.52
  89.9 0.1 copy.48
  90.0 0.1 mul.98
  90.1 0.1 broadcast_add_fusion
  90.2 38.1 %reduce-scatter.2.cloned.1.call-done = bf16[128,2048]{1,0:T(8,128)(2,1)} async-done(((bf16[512,2048]{1,0:T(8,128)(2,1)}), bf16[128,2048]{1,0:T(8,128)(2,1)}) %reduce-scatter.2.cloned.1.call-update) | async-done | bytes 524304 | tf_op jit(solution)/shard_map/reduce_scatter | solution.py:83
  128.4 1.5 multiply_reduce_fusion
  129.8 2.2 multiply_convert_fusion.1
  132.0 25.8 %scatter_custom_fusion = bf16[2048,2048]{1,0:T(8,128)(2,1)} fusion(s32[1024]{0:T(1024)S(1)} %bitcast.144, bf16[128,2048]{1,0:T(8,128)(2,1)} %multiply_convert_fusion.1, s32[1024]{0:T(1024)S(1)} %broadcast_clamp_fusion.1, bf16[]{:T(256)} %constant.67.clone.1), kind=kCustom, calls=%fused_computation.23 | custom fusion | bytes 8389120 | tf_op jit(solution)/shard_map/scatter | solution.py:106
  157.9 188.9 %all_to_all.10 = bf16[16,128,2048]{2,1,0:T(8,128)(2,1)S(1)} all-to-all(bf16[16,128,2048]{2,1,0:T(8,128)(2,1)} %bitcast.133), channel_id=1, replica_groups=mesh['replica'=2,'side'=4,'tp'=4] {'side','tp'}, dimensions={0} | all-to-all | bytes 16777216 | tf_op jit(solution)/shard_map/all_to_all | solution.py:109
  346.8 3.2 copy-done.2
  350.0 8.5 %fusion.23 = f32[2048,768]{1,0:T(8,128)} fusion(bf16[2048,2048]{1,0:T(8,128)(2,1)S(1)} %bitcast.135, bf16[1,2048,768]{2,1,0:T(8,128)(2,1)S(1)} %copy-done.10), kind=kOutput, calls=%fused_computation.34 | convolution fusion | flops 6442450944 | bytes 17825792 | tf_op jit(solution)/shard_map/dot_general | solution.py:112
  358.6 21.3 %convolution_convert_fusion = bf16[2048,2048]{1,0:T(8,128)(2,1)} fusion(f32[2048,768]{1,0:T(8,128)} %fusion.23, bf16[2048,2048]{1,0:T(8,128)(2,1)} %bitcast.136, bf16[1,768,2048]{2,1,0:T(8,128)(2,1)S(1)} %copy-done, bf16[1,2048,768]{2,1,0:T(8,128)(2,1)} %param.24), kind=kOutput, calls=%fused_computation.14 | convolution fusion | flops 12898533376 | bytes 29360128 | tf_op jit(solution)/shard_map/dot_general | solution.py:116
  379.8 5.2 all-to-all-start.1
  385.1 0.1 copy.47
  385.2 184.1 %all-to-all-done.1 = bf16[16,128,2048]{2,1,0:T(8,128)(2,1)} async-done(((bf16[16,128,2048]{2,1,0:T(8,128)(2,1)}), bf16[16,128,2048]{2,1,0:T(8,128)(2,1)}, u32[]{:S(2)}, u32[]{:S(2)}) %all-to-all-start.1) | async-done | bytes 8388640 | tf_op jit(solution)/shard_map/all_to_all | solution.py:115
  569.3 13.4 %gather_fusion = bf16[1024,2048]{1,0:T(8,128)(2,1)} fusion(bf16[2048,2048]{1,0:T(8,128)(2,1)} %bitcast.28, s32[1024]{0:T(1024)S(1)} %broadcast_clamp_fusion), kind=kCustom, calls=%fused_computation.5 | custom fusion | bytes 8392704 | tf_op jit(solution)/shard_map/gather | solution.py:124
  582.7 6.5 %fusion = f32[128,2048]{1,0:T(8,128)S(1)} fusion(bf16[1024,2048]{1,0:T(8,128)(2,1)} %gather_fusion, f32[128,8]{1,0:T(8,128)S(1)} %copy.47), kind=kLoop, calls=%fused_computation.8 | loop fusion | flops 6029312 | bytes 5246976 | tf_op jit(solution)/shard_map/reduce_sum | solution.py:127
  589.2 2.4 fusion.47
  (38 shorter events, 0.2 us)
Async XLA Ops:
  6.5 352.0 %copy-start = (bf16[1,768,2048]{2,1,0:T(8,128)(2,1)S(1)}, bf16[1,768,2048]{2,1,0:T(8,128)(2,1)}, u32[]{:S(2)}) copy-start(bf16[1,768,2048]{2,1,0:T(8,128)(2,1)} %param.25) | copy-start | bytes 9437188
  6.5 121.8 %reduce-scatter.2.cloned.1.call-start = ((), (), s32[]{:S(2)}) async-start(), calls=%async_computation.3 | async-start | bytes 2621440 | tf_op jit(solution)/shard_map/reduce_scatter | solution.py:83
  64.5 3.0 copy-start.4
  64.5 3.0 copy-start.5
  67.6 1.8 copy-start.3
  76.2 4.6 copy-start.9
  80.8 3.8 copy-start.6
  80.9 4.1 copy-start.8
  157.9 192.2 %copy-start.10 = (bf16[1,2048,768]{2,1,0:T(8,128)(2,1)S(1)}, bf16[1,2048,768]{2,1,0:T(8,128)(2,1)}, u32[]{:S(2)}) copy-start(bf16[1,2048,768]{2,1,0:T(8,128)(2,1)} %param.23) | copy-start | bytes 9437188
  346.8 3.2 copy-start.2
  379.8 5.2 copy-start.7
  379.8 189.4 %all-to-all-start.1 = ((bf16[16,128,2048]{2,1,0:T(8,128)(2,1)}), bf16[16,128,2048]{2,1,0:T(8,128)(2,1)}, u32[]{:S(2)}, u32[]{:S(2)}) async-start(bf16[16,128,2048]{2,1,0:T(8,128)(2,1)} %bitcast.134), calls=%async_computation.2 | async-start | bytes 16777216 | tf_op jit(solution)/shard_map/all_to_all | solution.py:115
  569.3 22.3 %copy-start.1 = (bf16[1,768,2048]{2,1,0:T(8,128)(2,1)S(1)}, bf16[1,768,2048]{2,1,0:T(8,128)(2,1)}, u32[]{:S(2)}) copy-start(bf16[1,768,2048]{2,1,0:T(8,128)(2,1)} %param.25) | copy-start | bytes 9437188
Sparse Core Ops, SparseCore 0:
  84.8 43.5 reduce-scatter.1
where the time goes:
time: 605 us; the launch traced here: 599 us
  waiting for transfers between devices  222 us (37%)
  blocking collectives  221 us (37%)
  local copies, waits for them, and re-layouts  68.8 us (11%)
  matrix products  46.1 us (8%)
  other arithmetic  21.1 us (3%)
  between operations  13.9 us (2%)
    all_to_all x1, blocking collectives, local(): lax.all_to_all(outgoing, ('side', 'tp'), split_axis=0, concat_axis=0, til...  189 us
    all_to_all x1, waiting for transfers between devices, local(): lax.all_to_all(jnp.dot(hidden, down_weight[0], preferred_element_type=jnp...  184 us
    reduce_scatter x1, waiting for transfers between devices, local(): lax.psum_scatter(jnp.dot(attended, out_weight, preferred_element_type=jnp...  38.1 us
    scatter x1, local copies, waits for them, and re-layouts, local(): jnp.zeros((experts_all * capacity, D), jnp.bfloat16).at[slot_index]  25.8 us
    dot_general x1, matrix products, local(): jnp.dot(hidden, down_weight[0], preferred_element_type=jnp.float32)  21.3 us
    all_gather x1, blocking collectives, local(): lax.all_gather(cache_keys, 'tp', axis=1, tiled=True)[0]  17.1 us
    all_gather x1, blocking collectives, local(): lax.all_gather(cache_values, 'tp', axis=1, tiled=True)[0]  15.4 us
    gather x1, local copies, waits for them, and re-layouts, local(): gathered = returned.reshape(experts_all * capacity, D)[slot_index]  13.4 us
  transfers between devices with their start and end apart: 2, of which 2 were waited for; matrix products, arithmetic and copies ran while one was open for 1% of the time, Pallas kernels for 0%

commit v1 on v0

--- a/solution.py
+++ b/solution.py
@@ -29,6 +29,26 @@
     return (highest, totals, context)
 
 
+def dense_experts(
+    stream, normed, gate_weight, up_weight, down_weight, expert_ids, numerators, experts_all
+):
+    weights = numerators.astype(jnp.float32)
+    weights = weights / jnp.sum(weights, axis=1, keepdims=True)
+    named = expert_ids[:, :, None] == jnp.arange(experts_all)[None, None, :]
+    per_expert = jnp.sum(jnp.where(named, weights[:, :, None], 0.0), axis=1)
+    all_weights = lax.all_gather(per_expert, ("side", "tp"), axis=0, tiled=True)
+    me = lax.axis_index(("side", "tp"))
+    own_weight = lax.dynamic_slice_in_dim(all_weights, me, 1, axis=1)
+    rows = lax.all_gather(normed, ("side", "tp"), axis=0, tiled=True)
+    gate_sum = jnp.dot(rows, gate_weight[0], preferred_element_type=jnp.float32)
+    upward = jnp.dot(rows, up_weight[0], preferred_element_type=jnp.float32)
+    hidden = (jax.nn.silu(gate_sum) * upward).astype(jnp.bfloat16)
+    expert_out = jnp.dot(hidden, down_weight[0], preferred_element_type=jnp.float32)
+    weighted = (expert_out * own_weight).astype(jnp.bfloat16)
+    mixture = lax.psum_scatter(weighted, ("side", "tp"), scatter_dimension=0, tiled=True)
+    return stream + mixture.astype(jnp.float32)
+
+
 def local(
     queries,
     new_keys,
@@ -56,8 +76,12 @@
         jnp.zeros((local_heads, group_rows), jnp.float32),
         jnp.zeros((local_heads, group_rows, HD), jnp.float32),
     )
-    key_piece = pick_heads(lax.all_gather(cache_keys, "tp", axis=1, tiled=True)[0], head_kv)
-    value_piece = pick_heads(lax.all_gather(cache_values, "tp", axis=1, tiled=True)[0], head_kv)
+    cache_both = lax.all_gather(
+        jnp.concatenate([cache_keys[0], cache_values[0]], axis=1), "tp", axis=0, tiled=True
+    )
+    key_width = cache_keys.shape[2]
+    key_piece = pick_heads(cache_both[:, :key_width], head_kv)
+    value_piece = pick_heads(cache_both[:, key_width:], head_kv)
     scores = (
         jnp.einsum("rhd,nhd->hrn", query_heads, key_piece, preferred_element_type=jnp.float32)
         * score_scale
@@ -96,6 +120,10 @@
     top_count = expert_ids.shape[1]
     copies = own_rows * top_count
     capacity = max(2, 2 * copies // experts_all)
+    if capacity >= own_rows:
+        return dense_experts(
+            stream, normed, gate_weight, up_weight, down_weight, expert_ids, numerators, experts_all
+        )
     flat_ids = expert_ids.reshape(copies)
     one_hot = (flat_ids[:, None] == jnp.arange(experts_all)[None, :]).astype(jnp.int32)
     earlier = jnp.cumsum(one_hot, axis=0) - one_hot

time: 605 us -> 340 us (0.56)
  blocking collectives: 221 us -> 32.8 us
  local copies, waits for them, and re-layouts: 68.8 us -> 27.6 us
  waiting for transfers between devices: 222 us -> 201 us
  other arithmetic: 21.1 us -> 10.3 us
  matrix products: 46.1 us -> 53.3 us
    all_to_all x1 -> x0, blocking collectives: 189 us -> none  [local(): lax.all_to_all(outgoing, ('side', 'tp'), split_axis=0, concat_axis=0, til...]
    all_to_all x1 -> x0, waiting for transfers between devices: 184 us -> none  [local(): lax.all_to_all(jnp.dot(hidden, down_weight[0], preferred_element_type=jnp...]
    reduce_scatter x0 -> x1, waiting for transfers between devices: none -> 103 us  [dense_experts(): lax.psum_scatter(weighted, ('side', 'tp'), scatter_dimension=0, tiled=True)]
    all_gather x0 -> x2, waiting for transfers between devices: none -> 55.9 us  [the longest x1 43.1 us: dense_experts(): rows = lax.all_gather(normed, ('side', 'tp'), axis=0, tiled=True)]
    scatter x1 -> x0, local copies, waits for them, and re-layouts: 25.8 us -> none  [local(): jnp.zeros((experts_all * capacity, D), jnp.bfloat16).at[slot_index]]
    gather x1 -> x0, local copies, waits for them, and re-layouts: 13.4 us -> none  [local(): gathered = returned.reshape(experts_all * capacity, D)[slot_index]]
    reduce_sum x3 -> x2, other arithmetic: 6.57 us -> 0.03 us  [the longest x1 0.02 us: dense_experts(): weights = weights / jnp.sum(weights, axis=1, keepdims=True)]
    all_gather x2 -> x1, blocking collectives: 32.5 us -> 32.8 us  [dense_experts(): all_weights = lax.all_gather(per_expert, ('side', 'tp'), axis=0, tiled=True)]
  transfers between devices with their start and end apart: 2 -> 4, of which waited for: 2 -> 4; matrix products, arithmetic and copies ran while one was open for 1% -> 6% of each run, Pallas kernels for 0% -> 0%
where the time goes in v1:
time: 340 us; the launch traced here: 339 us
  waiting for transfers between devices  201 us (59%)
  matrix products  53.3 us (16%)
  blocking collectives  32.8 us (10%)
  local copies, waits for them, and re-layouts  27.6 us (8%)
  between operations  13.3 us (4%)
  other arithmetic  10.3 us (3%)
    reduce_scatter x1, waiting for transfers between devices, dense_experts(): lax.psum_scatter(weighted, ('side', 'tp'), scatter_dimension=0, tiled=True)  103 us
    all_gather x1, waiting for transfers between devices, dense_experts(): rows = lax.all_gather(normed, ('side', 'tp'), axis=0, tiled=True)  43.1 us
    reduce_scatter x1, waiting for transfers between devices, local(): lax.psum_scatter(jnp.dot(attended, out_weight, preferred_element_type=jnp...  42.1 us
    all_gather x1, blocking collectives, dense_experts(): all_weights = lax.all_gather(per_expert, ('side', 'tp'), axis=0, tiled=True)  32.8 us
    dot_general x1, matrix products, dense_experts(): jnp.dot(hidden, down_weight[0], preferred_element_type=jnp.float32)  20.6 us
    all_gather x1, waiting for transfers between devices, local(): lax.all_gather(jnp.concatenate([cache_keys[0], cache_values[0]], axis=1),...  12.8 us
    dot_general x1, matrix products, dense_experts(): gate_sum = jnp.dot(rows, gate_weight[0], preferred_element_type=jnp.float32)  11.7 us
    gather x4, local copies, waits for them, and re-layouts, pick_heads(): return jnp.take(shaped, head_kv, axis=1)  10.9 us
  transfers between devices with their start and end apart: 4, of which 4 were waited for; matrix products, arithmetic and copies ran while one was open for 6% of the time, Pallas kernels for 0%

profile of v1, /device:TPU:0, one launch (start us, length us, event | category | flops | bytes accessed | tf_op | source)
XLA Modules:
  0.0 338.8 jit_solution(5835238811881287055)
XLA Ops:
  6.5 0.0 copy-start
  6.5 0.0 all-gather.3.cloned.1.call-start
  6.5 1.2 copy.44
  7.7 1.0 copy.45
  8.7 0.7 pad_maximum_fusion
  9.5 0.0 all-gather.3.cloned.1.call-update
  9.5 0.0 reduce-scatter.3.cloned.1.call-start
  9.6 2.0 copy.51
  11.6 2.0 copy.52
  13.6 2.0 copy.54
  15.7 2.0 copy.55
  17.8 2.7 gather_fusion.2
  20.5 2.7 gather_fusion.3
  23.2 0.1 iota_compare_fusion
  23.3 6.5 %fusion.5 = (f32[8,512]{1,0:T(8,128)S(1)}, f32[8,512,512]{2,1,0:T(8,128)}) fusion(pred[512,512]{0,1:T(8,128)(4,1)S(1)} %iota_compare_fusion, bf16[8,512,128]{2,1,0:T(8,128)(2,1)} %gather_fusion.2, pred[8]{0:T(512)(128)(4,1)S(1)} %compare_and_fusion, bf16[512,1024]{1,0:T(8,128)(2,1)} %param.15), kind=kOutput, calls=%fused_computation.14 | convolution fusion | flops 543682560 | bytes 10764296 | tf_op jit(solution)/shard_map/rhd,nhd->hrn/dot_general | solution.py:93
  29.8 12.8 %all-gather.3.cloned.1.call-done = bf16[512,1024]{0,1:T(8,128)(2,1)} async-done(((bf16[128,1024]{0,1:T(8,128)(2,1)}), bf16[512,1024]{0,1:T(8,128)(2,1)}) %all-gather.3.cloned.1.call-update) | async-done | bytes 1048592 | tf_op jit(solution)/shard_map/all_gather | solution.py:79
  42.6 2.2 fusion.63
  44.8 2.0 copy.48
  46.8 2.1 copy.46
  48.9 2.7 gather_fusion
  51.6 2.8 gather_fusion.1
  54.4 3.0 bitcast_reduce_fusion
  57.4 0.0 copy-done.1
  57.4 0.0 slice-start.1
  57.4 3.1 fusion.6
  60.5 0.0 slice-done.1
  60.5 3.2 fusion.1
  63.8 0.0 copy-start.5
  63.8 4.6 %fusion.23 = bf16[512,8,128]{0,2,1:T(8,128)(2,1)S(1)} fusion(f32[8,512,128]{1,2,0:T(8,128)} %fusion.6, f32[8,512,512]{2,1,0:T(8,128)S(1)} %bitcast.109, f32[8,512]{1,0:T(8,128)S(1)} %get-tuple-element.11, pred[512,512]{0,1:T(8,128)(4,1)S(1)} %iota_compare_fusion, bf16[8,512,128]{2,1,0:T(8,128)(2,1)} %gather_fusion.3, f32[512,8]{0,1:T(8,128)S(1)} %get-tuple-element.6, ...), kind=kOutput, calls=%fused_computation.32 | convolution fusion | flops 548405248 | bytes 12910600 | tf_op jit(solution)/shard_map/hrn,nhd->hrd/dot_general | solution.py:26
  68.4 0.0 copy-start.3
  68.4 0.0 copy-start.2
  68.5 0.0 copy-start.4
  68.5 3.8 %convolution_convert_fusion = bf16[512,2048]{1,0:T(8,128)(2,1)} fusion(bf16[512,1024]{0,1:T(8,128)(2,1)S(1)} %bitcast.117, bf16[1024,2048]{1,0:T(8,128)(2,1)S(1)} %copy-done.5), kind=kOutput, calls=%fused_computation.29 | convolution fusion | flops 2148532224 | bytes 7340032 | tf_op jit(solution)/shard_map/dot_general | solution.py:108
  72.3 0.0 reduce-scatter.3.cloned.1.call-update
  72.3 0.2 all-gather.5.cloned.1.call-start
  72.5 42.1 %reduce-scatter.3.cloned.1.call-done = bf16[128,2048]{1,0:T(8,128)(2,1)} async-done(((bf16[512,2048]{1,0:T(8,128)(2,1)}), bf16[128,2048]{1,0:T(8,128)(2,1)}) %reduce-scatter.3.cloned.1.call-update) | async-done | bytes 524304 | tf_op jit(solution)/shard_map/reduce_scatter | solution.py:107
  114.6 1.5 multiply_reduce_fusion
  116.1 2.2 multiply_convert_fusion.2
  118.3 0.0 all-gather.5.cloned.1.call-update
  118.3 0.0 reduce-scatter.5.cloned.1.call-start
  118.4 0.0 copy-done.2
  118.4 32.8 %all_gather.11 = f32[2048,16]{0,1:T(8,128)S(1)} all-gather(f32[128,16]{0,1:T(8,128)S(1)} %select_reduce_fusion), channel_id=1, replica_groups=mesh['replica'=2,'side'=4,'tp'=4] {'side','tp'}, dimensions={0}, use_global_device_ids=true | all-gather | bytes 139264 | tf_op jit(solution)/shard_map/all_gather | solution.py:39
  151.2 43.1 %all-gather.5.cloned.1.call-done = bf16[2048,2048]{1,0:T(8,128)(2,1)} async-done(((bf16[128,2048]{1,0:T(8,128)(2,1)}), bf16[2048,2048]{1,0:T(8,128)(2,1)}) %all-gather.5.cloned.1.call-update) | async-done | bytes 8388624 | tf_op jit(solution)/shard_map/all_gather | solution.py:42
  194.3 11.7 %fusion.19 = f32[2048,768]{1,0:T(8,128)} fusion(bf16[2048,2048]{1,0:T(8,128)(2,1)} %all-gather.5.cloned.1.call-done, bf16[1,2048,768]{2,1,0:T(8,128)(2,1)} %param.23), kind=kOutput, calls=%fused_computation.26 | convolution fusion | flops 6442450944 | bytes 17825792 | tf_op jit(solution)/shard_map/dot_general | solution.py:43
  206.0 20.6 %multiply_convert_fusion = bf16[2048,2048]{1,0:T(8,128)(2,1)} fusion(f32[2048]{0:T(1024)S(1)} %bitcast.116, f32[2048,768]{1,0:T(8,128)} %fusion.19, bf16[2048,2048]{1,0:T(8,128)(2,1)} %all-gather.5.cloned.1.call-done, bf16[1,768,2048]{2,1,0:T(8,128)(2,1)S(1)} %copy-done, bf16[1,2048,768]{2,1,0:T(8,128)(2,1)} %param.24), kind=kOutput, calls=%fused_computation.4 | convolution fusion | flops 12902727680 | bytes 29368320 | tf_op jit(solution)/shard_map/dot_general | solution.py:46
  226.6 0.0 reduce-scatter.5.cloned.1.call-update
  226.7 103.1 %reduce-scatter.5.cloned.1.call-done = bf16[128,2048]{1,0:T(8,128)(2,1)} async-done(((bf16[2048,2048]{1,0:T(8,128)(2,1)}), bf16[128,2048]{1,0:T(8,128)(2,1)}) %reduce-scatter.5.cloned.1.call-update) | async-done | bytes 524304 | tf_op jit(solution)/shard_map/reduce_scatter | solution.py:48
  329.7 2.5 convert_add_fusion
  (19 shorter events, 0.1 us)
Async XLA Ops:
  6.5 199.5 %copy-start = (bf16[1,768,2048]{2,1,0:T(8,128)(2,1)S(1)}, bf16[1,768,2048]{2,1,0:T(8,128)(2,1)}, u32[]{:S(2)}) copy-start(bf16[1,768,2048]{2,1,0:T(8,128)(2,1)} %param.25) | copy-start | bytes 9437188
  6.5 36.0 %all-gather.3.cloned.1.call-start = ((), (), s32[]{:S(2)}) async-start(), calls=%async_computation.2 | async-start | bytes 1310720 | tf_op jit(solution)/shard_map/all_gather | solution.py:79
  9.5 105.1 %reduce-scatter.3.cloned.1.call-start = ((), (), s32[]{:S(2)}) async-start(), calls=%async_computation.3 | async-start | bytes 2621440 | tf_op jit(solution)/shard_map/reduce_scatter | solution.py:107
  54.4 3.0 copy-start.1
  54.4 6.2 %slice-start = ((s8[8388608]{0:T(1024)(128)(4,1)}), s8[4194304]{0:T(1024)(128)(4,1)S(1)}, s32[]{:S(2)}) async-start(s8[8388608]{0:T(1024)(128)(4,1)} %bitcast.108), calls=%async_computation.6 | async-start | bytes 8388608
  57.4 3.1 slice-start.1
  63.8 4.6 %copy-start.5 = (bf16[1024,2048]{1,0:T(8,128)(2,1)S(1)}, bf16[1024,2048]{1,0:T(8,128)(2,1)}, u32[]{:S(2)}) copy-start(bf16[1024,2048]{1,0:T(8,128)(2,1)} %param.20) | copy-start | bytes 12582916
  68.4 4.1 %copy-start.3 = (bf16[2048]{0:T(1024)(128)(2,1)S(1)}, bf16[2048]{0:T(1024)(128)(2,1)}, u32[]{:S(2)}) copy-start(bf16[2048]{0:T(1024)(128)(2,1)} %param.22) | copy-start | bytes 12292
  68.4 49.9 %copy-start.2 = (s32[128,8]{0,1:T(8,128)S(1)}, s32[128,8]{0,1:T(8,128)}, u32[]{:S(2)}) copy-start(s32[128,8]{0,1:T(8,128)} %param.27) | copy-start | bytes 12292
  68.5 49.9 %copy-start.4 = (s32[128,8]{0,1:T(8,128)S(1)}, s32[128,8]{0,1:T(8,128)}, u32[]{:S(2)}) copy-start(s32[128,8]{0,1:T(8,128)} %param.26) | copy-start | bytes 12292
  72.3 122.1 %all-gather.5.cloned.1.call-start = ((), (), s32[]{:S(2)}) async-start(), calls=%async_computation.4 | async-start | bytes 8912896 | tf_op jit(solution)/shard_map/all_gather | solution.py:42
  118.3 211.4 %reduce-scatter.5.cloned.1.call-start = ((), (), s32[]{:S(2)}) async-start(), calls=%async_computation.5 | async-start | bytes 8912896 | tf_op jit(solution)/shard_map/reduce_scatter | solution.py:48
Sparse Core Ops, SparseCore 0:
  9.6 32.8 all-gather.2
  72.4 42.1 reduce-scatter.2
  118.4 75.8 all-gather.4
  226.8 102.8 reduce-scatter.4

commit v2 on v1

--- a/solution.py
+++ b/solution.py
@@ -1,14 +1,18 @@
+import functools
 import math
 
 import jax
 import jax.numpy as jnp
 from jax import lax
+from jax.experimental import pallas as pl
+from jax.experimental.pallas import tpu as pltpu
 from jax.sharding import PartitionSpec as P
 
 D = 2048
 H = 32
 KV = 4
 HD = 128
+MESH = pl.DeviceIdType.MESH
 
 
 def pick_heads(block_rows, head_kv):
@@ -27,6 +31,271 @@
         "hrn,nhd->hrd", exponent.astype(jnp.bfloat16), values, preferred_element_type=jnp.float32
     )
     return (highest, totals, context)
+
+
+def piece(length, most):
+    return most if length % most == 0 else length
+
+
+def near_first(at, step, count):
+    found = jnp.int32(0)
+    for place in range(count):
+        order = sorted(range(count), key=lambda other: (abs(other - place), other))
+        for turn in range(count):
+            hit = jnp.logical_and(at == place, step == turn)
+            found = found + jnp.where(hit, order[turn], 0)
+    return found
+
+
+def experts_kernel(
+    side_count, tp_count, own_ref, weight_ref, gate_hbm, up_hbm, down_hbm, mix_ref,
+    rows, parts, from_core, from_y, from_z, gate, up, down, hidden,
+    load_sem, row_recv, up_send, down_send, y_send, core_send,
+    core1_send, core1_recv, y1_send, y1_recv, z1_send, z1_recv,
+):
+    side, z = lax.axis_index("side"), lax.axis_index("tp")
+    y, core = side // 2, side % 2
+    other_y, other_core = side + 2 - 4 * y, side + 1 - 2 * core
+    far_core = other_y + 1 - 2 * core
+    own_rows, width = own_ref.shape
+    inner = gate.shape[1]
+    loads = [
+        pltpu.make_async_copy(source.at[0], target, load_sem.at[at])
+        for at, (source, target) in enumerate(((gate_hbm, gate), (up_hbm, up), (down_hbm, down)))
+    ]
+    for load in loads:
+        load.start()
+
+    barrier = pltpu.get_barrier_semaphore()
+    for step in range(1, tp_count):
+        pl.semaphore_signal(
+            barrier, inc=1, device_id={"tp": lax.rem(z + step, tp_count)}, device_id_type=MESH
+        )
+    for target in (other_y, other_core):
+        pl.semaphore_signal(barrier, inc=1, device_id={"side": target}, device_id_type=MESH)
+    pl.semaphore_wait(barrier, tp_count + 1)
+
+    def send_row(at_side, at_z, send_sem, target):
+        return pltpu.make_async_remote_copy(
+            src_ref=rows.at[at_side, at_z],
+            dst_ref=rows.at[at_side, at_z],
+            send_sem=send_sem,
+            recv_sem=row_recv.at[at_side, at_z],
+            device_id=target,
+            device_id_type=MESH,
+        )
+
+    def wait_row(at_side, at_z):
+        send_row(at_side, at_z, up_send.at[at_z], {"side": other_core}).wait_recv()
+
+    def line_sends(at_z):
+        return (
+            (
+                jnp.logical_and(at_z <= z, z < tp_count - 1),
+                send_row(side, at_z, up_send.at[at_z], {"tp": jnp.minimum(z + 1, tp_count - 1)}),
+            ),
+            (
+                jnp.logical_and(at_z >= z, z > 0),
+                send_row(side, at_z, down_send.at[at_z], {"tp": jnp.maximum(z - 1, 0)}),
+            ),
+        )
+
+    def side_sends(at_z):
+        return (
+            send_row(side, at_z, y_send.at[at_z], {"side": other_y}),
+            send_row(side, at_z, core_send.at[0, at_z], {"side": other_core}),
+        )
+
+    def pass_on(at_z):
+        return send_row(other_y, at_z, core_send.at[1, at_z], {"side": other_core})
+
+    def spread(at_z):
+        for condition, copy in line_sends(at_z):
+            pl.when(condition)(copy.start)
+        for copy in side_sends(at_z):
+            copy.start()
+
+    def to_core(at_y, at_z):
+        return pltpu.make_async_remote_copy(
+            src_ref=parts.at[2 * at_y + 1 - core, at_z],
+            dst_ref=from_core.at[at_y, at_z],
+            send_sem=core1_send.at[at_y, at_z],
+            recv_sem=core1_recv.at[at_y, at_z],
+            device_id={"side": other_core},
+            device_id_type=MESH,
+        )
+
+    def to_y(at_z):
+        return pltpu.make_async_remote_copy(
+            src_ref=parts.at[other_y, at_z],
+            dst_ref=from_y.at[at_z],
+            send_sem=y1_send.at[at_z],
+            recv_sem=y1_recv.at[at_z],
+            device_id={"side": other_y},
+            device_id_type=MESH,
+        )
+
+    def to_line(at_z, slot, target):
+        return pltpu.make_async_remote_copy(
+            src_ref=parts.at[side, at_z],
+            dst_ref=from_z.at[slot],
+            send_sem=z1_send.at[at_z],
+            recv_sem=z1_recv.at[slot],
+            device_id={"tp": target},
+            device_id_type=MESH,
+        )
+
+    def add_to_part(at_side, at_z, arrived):
+        parts[at_side, at_z] = (
+            parts[at_side, at_z].astype(jnp.float32) + arrived[...].astype(jnp.float32)
+        ).astype(jnp.bfloat16)
+
+    rows[side, z] = own_ref[...]
+    spread(z)
+    for load in loads:
+        load.wait()
+
+    def forward(step, carry):
+        at_z = near_first(z, step, tp_count)
+
+        @pl.when(step + 1 < tp_count)
+        def _():
+            next_z = near_first(z, step + 1, tp_count)
+            wait_row(side, next_z)
+            spread(next_z)
+
+        wait_row(other_y, at_z)
+        pass_on(at_z).start()
+        wait_row(other_core, at_z)
+        wait_row(far_core, at_z)
+        count = side_count * own_rows
+        block = piece(inner, 256)
+
+        def hide(at, carry):
+            columns = pl.ds(pl.multiple_of(at * block, block), block)
+            taken = rows[:, at_z].reshape(count, width)
+            gate_sum = jnp.dot(taken, gate[:, columns], preferred_element_type=jnp.float32)
+            upward = jnp.dot(taken, up[:, columns], preferred_element_type=jnp.float32)
+            hidden[:, columns] = (gate_sum / (1.0 + jnp.exp(-gate_sum)) * upward).astype(
+                jnp.bfloat16
+            )
+            return carry
+
+        lax.fori_loop(0, inner // block, hide, 0)
+        out_block = piece(width, 512)
+
+        def show(at, carry):
+            columns = pl.ds(pl.multiple_of(at * out_block, out_block), out_block)
+            out = jnp.dot(hidden[...], down[:, columns], preferred_element_type=jnp.float32)
+            scale = weight_ref[:, at_z].reshape(count, 1)
+            parts[:, at_z, :, columns] = (
+                (out * scale).astype(jnp.bfloat16).reshape(side_count, own_rows, out_block)
+            )
+            return carry
+
+        lax.fori_loop(0, width // out_block, show, 0)
+        for at_y in range(side_count // 2):
+            to_core(at_y, at_z).start()
+        return carry
+
+    lax.fori_loop(0, tp_count, forward, 0)
+
+    def back_y(step, carry):
+        at_z = near_first(z, tp_count - 1 - step, tp_count)
+        to_core(1 - y, at_z).wait_recv()
+        add_to_part(other_y, at_z, from_core.at[1 - y, at_z])
+        to_y(at_z).start()
+        to_core(y, at_z).wait_recv()
+        add_to_part(side, at_z, from_core.at[y, at_z])
+        return carry
+
+    lax.fori_loop(0, tp_count, back_y, 0)
+
+    def back_z(step, carry):
+        at_z = near_first(z, tp_count - 1 - step, tp_count)
+        to_y(at_z).wait_recv()
+        add_to_part(side, at_z, from_y.at[at_z])
+        to_line(at_z, z, at_z).start()
+        return carry
+
+    lax.fori_loop(0, tp_count - 1, back_z, 0)
+    to_y(z).wait_recv()
+    mix_ref[...] = parts[side, z].astype(jnp.float32) + from_y[z].astype(jnp.float32)
+
+    def collect(step, carry):
+        at_z = near_first(z, step, tp_count)
+        to_line(at_z, at_z, at_z).wait_recv()
+        mix_ref[...] += from_z[at_z].astype(jnp.float32)
+        return carry
+
+    lax.fori_loop(1, tp_count, collect, 0)
+
+    def drain(at_z, carry):
+        for condition, copy in line_sends(at_z):
+            pl.when(condition)(copy.wait_send)
+        for copy in side_sends(at_z):
+            copy.wait_send()
+        pass_on(at_z).wait_send()
+        for at_y in range(side_count // 2):
+            to_core(at_y, at_z).wait_send()
+        to_y(at_z).wait_send()
+        pl.when(at_z != z)(to_line(at_z, z, at_z).wait_send)
+        return carry
+
+    lax.fori_loop(0, tp_count, drain, 0)
+
+
+def exchange_experts(normed, own_weight, gate_weight, up_weight, down_weight):
+    side_count, tp_count = lax.axis_size("side"), lax.axis_size("tp")
+    own_rows, width = normed.shape
+    inner = gate_weight.shape[2]
+    half = side_count // 2
+    dma = pltpu.SemaphoreType.DMA
+    block = (own_rows, width)
+    flops = 6 * side_count * tp_count * own_rows * width * inner
+    return pl.pallas_call(
+        functools.partial(experts_kernel, side_count, tp_count),
+        out_shape=jax.ShapeDtypeStruct(block, jnp.float32),
+        in_specs=[pl.BlockSpec(memory_space=pltpu.VMEM)] * 2
+        + [pl.BlockSpec(memory_space=pl.ANY)] * 3,
+        out_specs=pl.BlockSpec(memory_space=pltpu.VMEM),
+        scratch_shapes=[
+            pltpu.VMEM((side_count, tp_count) + block, jnp.bfloat16),
+            pltpu.VMEM((side_count, tp_count) + block, jnp.bfloat16),
+            pltpu.VMEM((half, tp_count) + block, jnp.bfloat16),
+            pltpu.VMEM((tp_count,) + block, jnp.bfloat16),
+            pltpu.VMEM((tp_count,) + block, jnp.bfloat16),
+            pltpu.VMEM((width, inner), jnp.bfloat16),
+            pltpu.VMEM((width, inner), jnp.bfloat16),
+            pltpu.VMEM((inner, width), jnp.bfloat16),
+            pltpu.VMEM((side_count * own_rows, inner), jnp.bfloat16),
+            dma((3,)),
+            dma((side_count, tp_count)),
+            dma((tp_count,)),
+            dma((tp_count,)),
+            dma((tp_count,)),
+            dma((2, tp_count)),
+            dma((half, tp_count)),
+            dma((half, tp_count)),
+            dma((tp_count,)),
+            dma((tp_count,)),
+            dma((tp_count,)),
+            dma((tp_count,)),
+        ],
+        compiler_params=pltpu.CompilerParams(
+            collective_id=0, has_side_effects=True, vmem_limit_bytes=58 * 2**20
+        ),
+        cost_estimate=pl.CostEstimate(
+            flops=flops, bytes_accessed=6 * width * inner, transcendentals=0
+        ),
+        name="experts_exchange",
+    )(
+        normed,
+        own_weight.reshape(side_count, tp_count, own_rows, 1),
+        gate_weight,
+        up_weight,
+        down_weight,
+    )
 
 
 def dense_experts(
@@ -39,6 +308,8 @@
     all_weights = lax.all_gather(per_expert, ("side", "tp"), axis=0, tiled=True)
     me = lax.axis_index(("side", "tp"))
     own_weight = lax.dynamic_slice_in_dim(all_weights, me, 1, axis=1)
+    if lax.axis_size("side") == 4:
+        return stream + exchange_experts(normed, own_weight, gate_weight, up_weight, down_weight)
     rows = lax.all_gather(normed, ("side", "tp"), axis=0, tiled=True)
     gate_sum = jnp.dot(rows, gate_weight[0], preferred_element_type=jnp.float32)
     upward = jnp.dot(rows, up_weight[0], preferred_element_type=jnp.float32)

time: 340 us -> 250 us (0.74)
  waiting for transfers between devices: 201 us -> 30.1 us
  Pallas kernels: 0 us -> 122 us
  matrix products: 53.3 us -> 24.1 us
  local copies, waits for them, and re-layouts: 27.6 us -> 12.3 us
    pallas_call x0 -> x1, Pallas kernels: none -> 122 us  [exchange_experts(): pl.pallas_call(functools.partial(experts_kernel, side_count, tp_count), o...]
    reduce_scatter x1 -> x0, waiting for transfers between devices: 103 us -> none  [dense_experts(): lax.psum_scatter(weighted, ('side', 'tp'), scatter_dimension=0, tiled=True)]
    all_gather x1 -> x0, waiting for transfers between devices: 43.1 us -> none  [dense_experts(): rows = lax.all_gather(normed, ('side', 'tp'), axis=0, tiled=True)]
    reduce_scatter x1, waiting for transfers between devices: 42.1 us -> 7.68 us  [local(): lax.psum_scatter(jnp.dot(attended, out_weight, preferred_element_type=jnp...]
    dot_general x2 -> x0, matrix products: 32.3 us -> none  [the longest x1 20.6 us: dense_experts(): jnp.dot(hidden, down_weight[0], preferred_element_type=jnp.float32)]
    all_gather x1, waiting for transfers between devices: 12.8 us -> 22.4 us  [local(): lax.all_gather(jnp.concatenate([cache_keys[0], cache_values[0]], axis=1),...]
    reshape x4, local copies, waits for them, and re-layouts: 8.21 us -> 1.08 us  [pick_heads(): shaped = block_rows.reshape(length_now, KV, HD)]
    gather x4, local copies, waits for them, and re-layouts: 10.9 us -> 3.91 us  [pick_heads(): return jnp.take(shaped, head_kv, axis=1)]
  transfers between devices with their start and end apart: 4 -> 2, of which waited for: 4 -> 2; matrix products, arithmetic and copies ran while one was open for 6% -> 5% of each run, Pallas kernels for 0% -> 0%
where the time goes in v2:
time: 250 us
  Pallas kernels  122 us (49%)
  blocking collectives  35.1 us (14%)
  waiting for transfers between devices  30.1 us (12%)
  matrix products  24.1 us (10%)
  between operations  13.7 us (5%)
  local copies, waits for them, and re-layouts  12.3 us (5%)
  other arithmetic  12.3 us (5%)
    pallas_call x1, Pallas kernels, exchange_experts(): pl.pallas_call(functools.partial(experts_kernel, side_count, tp_count), o...  122 us
    all_gather x1, blocking collectives, dense_experts(): all_weights = lax.all_gather(per_expert, ('side', 'tp'), axis=0, tiled=True)  35.1 us
    all_gather x1, waiting for transfers between devices, local(): lax.all_gather(jnp.concatenate([cache_keys[0], cache_values[0]], axis=1),...  22.4 us
    dot_general x2, matrix products, softmax_update(): jnp.einsum('hrn,nhd->hrd', exponent.astype(jnp.bfloat16), values, preferr...  10.9 us
    reduce_scatter x1, waiting for transfers between devices, local(): lax.psum_scatter(jnp.dot(attended, out_weight, preferred_element_type=jnp...  7.68 us
    reduce_sum x1, other arithmetic, softmax_update(): totals = totals * factor + jnp.sum(exponent, axis=-1)  5.66 us
  transfers between devices with their start and end apart: 2, of which 2 were waited for; matrix products, arithmetic and copies ran while one was open for 5% of the time, Pallas kernels for 0%

profile of v2, /device:TPU:0, one launch (start us, length us, event | category | flops | bytes accessed | tf_op | source)
XLA Modules:
  0.0 249.8 jit_solution(13458567981426528762)
XLA Ops:
  6.5 0.0 copy-start
  6.5 0.0 all-gather.2.cloned.1.call-start
  6.5 1.1 copy.46
  7.7 1.0 copy.47
  8.7 0.7 pad_maximum_fusion
  9.4 0.0 all-gather.2.cloned.1.call-update
  9.4 0.0 reduce-scatter.2.cloned.1.call-start
  9.5 1.3 copy.53
  10.7 0.3 copy.54
  11.0 1.3 copy.56
  12.3 0.3 copy.57
  12.6 0.7 gather_fusion.2
  13.4 1.7 gather_fusion.3
  15.0 0.1 iota_compare_fusion
  15.1 0.0 copy-done
  15.1 5.0 %fusion.5 = (f32[8,512]{1,0:T(8,128)S(1)}, f32[8,512,512]{2,1,0:T(8,128)}) fusion(pred[512,512]{0,1:T(8,128)(4,1)S(1)} %iota_compare_fusion, bf16[8,512,128]{2,1,0:T(8,128)(2,1)S(1)} %gather_fusion.2, pred[8]{0:T(512)(128)(4,1)S(1)} %compare_and_fusion, bf16[512,1024]{1,0:T(8,128)(2,1)S(1)} %copy-done), kind=kOutput, calls=%fused_computation.13 | convolution fusion | flops 543682560 | bytes 10764296 | tf_op jit(solution)/shard_map/rhd,nhd->hrn/dot_general | solution.py:364
  20.1 22.4 %all-gather.2.cloned.1.call-done = bf16[512,1024]{0,1:T(8,128)(2,1)} async-done(((bf16[128,1024]{0,1:T(8,128)(2,1)}), bf16[512,1024]{0,1:T(8,128)(2,1)}) %all-gather.2.cloned.1.call-update) | async-done | bytes 1048592 | tf_op jit(solution)/shard_map/all_gather | solution.py:350
  42.5 1.3 fusion.57
  43.8 0.3 copy.48
  44.0 0.8 gather_fusion
  44.8 4.5 %bitcast_reduce_fusion = (f32[8,512]{1,0:T(8,128)S(1)}, f32[8,512,512]{2,1,0:T(8,128)}) fusion(bf16[8,512,128]{2,1,0:T(8,128)(2,1)S(1)} %gather_fusion, pred[8]{0:T(512)(128)(4,1)S(1)} %compare_and_fusion, bf16[512,1024]{1,0:T(8,128)(2,1)S(1)} %copy-done), kind=kOutput, calls=%fused_computation.6 | convolution fusion | flops 541585408 | bytes 10502152 | tf_op jit(solution)/shard_map/rhd,nhd->hrn/dot_general | solution.py:357
  49.3 0.3 copy.50
  49.6 0.8 gather_fusion.1
  50.3 0.0 copy-start.1
  50.4 0.0 slice-start
  50.4 6.6 %fusion.6 = f32[8,512,128]{1,2,0:T(8,128)} fusion(f32[8,512,512]{2,1,0:T(8,128)} %get-tuple-element.16, f32[8,512]{1,0:T(8,128)S(1)} %get-tuple-element.12, bf16[8,512,128]{2,1,0:T(8,128)(2,1)S(1)} %gather_fusion.1, pred[8]{0:T(512)(128)(4,1)S(1)} %compare_and_fusion), kind=kOutput, calls=%fused_computation.14 | convolution fusion | flops 543686656 | bytes 11550728 | tf_op jit(solution)/shard_map/hrn,nhd->hrd/dot_general | solution.py:30
  57.0 0.0 copy-done.1
  57.0 5.7 %fusion.1 = (f32[8,512]{1,0:T(8,128)S(1)}, f32[8,512]{1,0:T(8,128)S(1)}) fusion(f32[8,512,512]{2,1,0:T(8,128)} %get-tuple-element.14, f32[8,512]{1,0:T(8,128)S(1)} %get-tuple-element.11, pred[512,512]{0,1:T(8,128)(4,1)S(1)} %iota_compare_fusion, f32[8,512]{1,0:T(8,128)S(1)} %get-tuple-element.12, f32[8,512,512]{2,1,0:T(8,128)S(1)} %copy-done.1), kind=kLoop, calls=%fused_computation.9 | loop fusion | flops 14671872 | bytes 17104896 | tf_op jit(solution)/shard_map/reduce_sum | solution.py:29
  62.7 0.0 slice-done
  62.7 0.0 slice-done.1
  62.7 0.0 copy-done.4
  62.7 0.0 copy-start.8
  62.7 4.3 %fusion.17 = bf16[512,8,128]{0,2,1:T(8,128)(2,1)S(1)} fusion(f32[8,512,128]{1,2,0:T(8,128)S(1)} %copy-done.4, f32[8,512,512]{2,1,0:T(8,128)S(1)} %bitcast.97, f32[8,512]{1,0:T(8,128)S(1)} %get-tuple-element.11, pred[512,512]{0,1:T(8,128)(4,1)S(1)} %iota_compare_fusion, bf16[8,512,128]{2,1,0:T(8,128)(2,1)} %gather_fusion.3, ...), kind=kOutput, calls=%fused_computation.25 | convolution fusion | flops 548405248 | bytes 12910600 | tf_op jit(solution)/shard_map/hrn,nhd->hrd/dot_general | solution.py:30
  67.0 0.0 copy-start.6
  67.0 0.0 copy-start.5
  67.1 0.0 copy-start.7
  67.1 0.0 copy-done.8
  67.1 0.0 copy-start.2
  67.1 3.8 %convolution_convert_fusion = bf16[512,2048]{1,0:T(8,128)(2,1)} fusion(bf16[512,1024]{0,1:T(8,128)(2,1)S(1)} %bitcast.105, bf16[1024,2048]{1,0:T(8,128)(2,1)S(1)} %copy-done.8), kind=kOutput, calls=%fused_computation.22 | convolution fusion | flops 2148532224 | bytes 7340032 | tf_op jit(solution)/shard_map/dot_general | solution.py:379
  70.9 0.0 reduce-scatter.2.cloned.1.call-update
  70.9 0.0 copy-done.5
  71.0 35.1 %all_gather.7 = f32[2048,16]{0,1:T(8,128)S(1)} all-gather(f32[128,16]{0,1:T(8,128)S(1)} %select_reduce_fusion), channel_id=1, replica_groups=mesh['replica'=2,'side'=4,'tp'=4] {'side','tp'}, dimensions={0}, use_global_device_ids=true | all-gather | bytes 139264 | tf_op jit(solution)/shard_map/all_gather | solution.py:308
  106.1 1.3 copy.60.weight_ref
  107.4 7.7 %reduce-scatter.2.cloned.1.call-done = bf16[128,2048]{1,0:T(8,128)(2,1)} async-done(((bf16[512,2048]{1,0:T(8,128)(2,1)}), bf16[128,2048]{1,0:T(8,128)(2,1)}) %reduce-scatter.2.cloned.1.call-update) | async-done | bytes 524304 | tf_op jit(solution)/shard_map/reduce_scatter | solution.py:378
  115.1 1.3 multiply_reduce_fusion
  116.4 2.1 multiply_convert_fusion.own_ref
  118.5 122.2 %experts_exchange.1 = f32[128,2048]{1,0:T(8,128)} custom-call(bf16[128,2048]{1,0:T(8,128)(2,1)} %multiply_convert_fusion.own_ref, f32[4,4,128,1]{3,2,1,0:T(8,128)} %copy.60.weight_ref, bf16[1,2048,768]{2,1,0:T(8,128)(2,1)} %gate_hbm.1, bf16[1,2048,768]{2,1,0:T(8,128)(2,1)} %up_hbm.1, bf16[1,768,2048]{2,1,0:T(8,128)(2,1)} %down_hbm.1), custom_call_target="tpu_custom_call" | custom-call | flops 19327352832 | bytes 9437184 | tf_op jit(solution)/shard_map/experts_exchange/pallas_call | solution.py:256
  240.6 2.4 fusion.37
  (19 shorter events, 0.1 us)
Async XLA Ops:
  6.5 8.6 %copy-start = (bf16[512,1024]{1,0:T(8,128)(2,1)S(1)}, bf16[512,1024]{1,0:T(8,128)(2,1)}, u32[]{:S(2)}) copy-start(bf16[512,1024]{1,0:T(8,128)(2,1)} %param.15) | copy-start | bytes 3145732
  6.5 35.9 %all-gather.2.cloned.1.call-start = ((), (), s32[]{:S(2)}) async-start(), calls=%async_computation.1 | async-start | bytes 1310720 | tf_op jit(solution)/shard_map/all_gather | solution.py:350
  9.4 105.7 %reduce-scatter.2.cloned.1.call-start = ((), (), s32[]{:S(2)}) async-start(), calls=%async_computation.2 | async-start | bytes 2621440 | tf_op jit(solution)/shard_map/reduce_scatter | solution.py:378
  50.3 6.6 %copy-start.1 = (f32[8,512,512]{2,1,0:T(8,128)S(1)}, f32[8,512,512]{2,1,0:T(8,128)}, u32[]{:S(2)}) copy-start(f32[8,512,512]{2,1,0:T(8,128)} %get-tuple-element.16) | copy-start | bytes 25165828
  50.4 12.3 %slice-start = ((s8[8388608]{0:T(1024)(128)(4,1)}), s8[4194304]{0:T(1024)(128)(4,1)S(1)}, s32[]{:S(2)}) async-start(s8[8388608]{0:T(1024)(128)(4,1)} %bitcast.96), calls=%async_computation.3 | async-start | bytes 8388608
  57.0 5.7 %slice-start.1 = ((s8[8388608]{0:T(1024)(128)(4,1)}), s8[4194304]{0:T(1024)(128)(4,1)S(1)}, s32[]{:S(2)}) async-start(s8[8388608]{0:T(1024)(128)(4,1)} %bitcast.96), calls=%async_computation.4 | async-start | bytes 8388608
  57.0 5.7 %copy-start.4 = (f32[8,512,128]{1,2,0:T(8,128)S(1)}, f32[8,512,128]{1,2,0:T(8,128)}, u32[]{:S(2)}) copy-start(f32[8,512,128]{1,2,0:T(8,128)} %fusion.6) | copy-start | bytes 6291460
  62.7 4.3 %copy-start.8 = (bf16[1024,2048]{1,0:T(8,128)(2,1)S(1)}, bf16[1024,2048]{1,0:T(8,128)(2,1)}, u32[]{:S(2)}) copy-start(bf16[1024,2048]{1,0:T(8,128)(2,1)} %param.20) | copy-start | bytes 12582916
  67.0 3.9 %copy-start.6 = (bf16[2048]{0:T(1024)(128)(2,1)S(1)}, bf16[2048]{0:T(1024)(128)(2,1)}, u32[]{:S(2)}) copy-start(bf16[2048]{0:T(1024)(128)(2,1)} %param.22) | copy-start | bytes 12292
  67.0 3.9 %copy-start.5 = (s32[128,8]{0,1:T(8,128)S(1)}, s32[128,8]{0,1:T(8,128)}, u32[]{:S(2)}) copy-start(s32[128,8]{0,1:T(8,128)} %param.27) | copy-start | bytes 12292
  67.1 3.9 %copy-start.7 = (s32[128,8]{0,1:T(8,128)S(1)}, s32[128,8]{0,1:T(8,128)}, u32[]{:S(2)}) copy-start(s32[128,8]{0,1:T(8,128)} %param.26) | copy-start | bytes 12292
  67.1 48.0 %copy-start.2 = (bf16[128,2048]{1,0:T(8,128)(2,1)S(1)}, bf16[128,2048]{1,0:T(8,128)(2,1)}, u32[]{:S(2)}) copy-start(bf16[128,2048]{1,0:T(8,128)(2,1)} %param.21) | copy-start | bytes 1572868
  118.5 122.2 %copy-start.3 = (bf16[128,2048]{1,0:T(8,128)(2,1)S(1)}, bf16[128,2048]{1,0:T(8,128)(2,1)}, u32[]{:S(2)}) copy-start(bf16[128,2048]{1,0:T(8,128)(2,1)} %reduce-scatter.2.cloned.1.call-done) | copy-start | bytes 1572868
Sparse Core Ops, SparseCore 0:
  9.6 32.8 all-gather.1
  71.0 44.0 reduce-scatter.1

commit v3 on v2

--- a/solution.py
+++ b/solution.py
@@ -45,6 +45,240 @@
             hit = jnp.logical_and(at == place, step == turn)
             found = found + jnp.where(hit, order[turn], 0)
     return found
+
+
+def attend_kernel(
+    tp_count, q_ref, new_k, new_v, cache_k, cache_v, out_hbm, residual_ref, gain_ref,
+    stream_ref, normed_ref,
+    keys, values, out_w, context, parts, from_below, from_above,
+    load_sem, key_send, key_recv, value_send, value_recv, part_send, below_recv, above_recv,
+):
+    z = lax.axis_index("tp")
+    top = tp_count - 1
+    group_rows = q_ref.shape[0]
+    local_heads = q_ref.shape[1] // HD
+    own_rows = residual_ref.shape[0]
+    cached = cache_k.shape[1]
+    cache_len = cached * tp_count
+    spot = pl.ds(pl.multiple_of(z * cached, cached), cached)
+
+    def head_of(at):
+        return pl.ds(pl.multiple_of(at * HD, HD), HD)
+
+    tail = pl.ds(cache_len, group_rows)
+    pairs = (
+        (new_k.at[:, head_of(z)], keys.at[tail]),
+        (new_v.at[:, head_of(z)], values.at[tail]),
+        (cache_k.at[0, :, head_of(z)], keys.at[spot]),
+        (cache_v.at[0, :, head_of(z)], values.at[spot]),
+        (out_hbm, out_w),
+    )
+    loads = [
+        pltpu.make_async_copy(source, target, load_sem.at[at])
+        for at, (source, target) in enumerate(pairs)
+    ]
+    for load in loads:
+        load.start()
+
+    barrier = pltpu.get_barrier_semaphore()
+    for step in range(1, tp_count):
+        pl.semaphore_signal(
+            barrier, inc=1, device_id={"tp": lax.rem(z + step, tp_count)}, device_id_type=MESH
+        )
+    pl.semaphore_wait(barrier, top)
+
+    def give(source, target, at, start, send_sem, recv_sem):
+        return pltpu.make_async_remote_copy(
+            src_ref=source.at[0, :, head_of(at)],
+            dst_ref=target.at[pl.ds(pl.multiple_of(start * cached, cached), cached)],
+            send_sem=send_sem.at[at],
+            recv_sem=recv_sem.at[start],
+            device_id={"tp": at},
+            device_id_type=MESH,
+        )
+
+    def gives(at, start):
+        return (
+            give(cache_k, keys, at, start, key_send, key_recv),
+            give(cache_v, values, at, start, value_send, value_recv),
+        )
+
+    for step in range(1, tp_count):
+        for copy in gives(lax.rem(z + step, tp_count), z):
+            copy.start()
+
+    def climb(at, target):
+        return pltpu.make_async_remote_copy(
+            src_ref=parts.at[at],
+            dst_ref=from_below.at[at],
+            send_sem=part_send.at[at],
+            recv_sem=below_recv.at[at],
+            device_id={"tp": target},
+            device_id_type=MESH,
+        )
+
+    def descend(at, target):
+        return pltpu.make_async_remote_copy(
+            src_ref=parts.at[at],
+            dst_ref=from_above.at[at],
+            send_sem=part_send.at[at],
+            recv_sem=above_recv.at[at],
+            device_id={"tp": target},
+            device_id_type=MESH,
+        )
+
+    above, below = jnp.minimum(z + 1, top), jnp.maximum(z - 1, 0)
+    for load in loads:
+        load.wait()
+    for step in range(1, tp_count):
+        peer = lax.rem(z + step, tp_count)
+        for copy in gives(peer, peer):
+            copy.wait_recv()
+
+    score_scale = 1.0 / math.sqrt(HD)
+
+    def project(step, carry):
+        at = near_first(z, top - step, tp_count)
+        own = pl.ds(pl.multiple_of(at * own_rows, own_rows), own_rows)
+        shape = (own_rows, cache_len + group_rows)
+        column = lax.broadcasted_iota(jnp.int32, shape, 1)
+        position = lax.broadcasted_iota(jnp.int32, shape, 0) + at * own_rows
+        visible = column <= position + cache_len
+        for head in range(local_heads):
+            lanes = pl.ds(head * HD, HD)
+            scores = lax.dot_general(
+                q_ref[own, lanes],
+                keys[...],
+                (((1,), (1,)), ((), ())),
+                preferred_element_type=jnp.float32,
+            )
+            scores = jnp.where(visible, scores * score_scale, -1e30)
+            exponent = jnp.exp(scores - jnp.max(scores, axis=-1, keepdims=True))
+            totals = jnp.sum(exponent, axis=-1, keepdims=True)
+            mixed = jnp.dot(
+                exponent.astype(jnp.bfloat16), values[...], preferred_element_type=jnp.float32
+            )
+            context[:, lanes] = (mixed / totals).astype(jnp.bfloat16)
+        parts[at] = jnp.dot(
+            context[...], out_w[...], preferred_element_type=jnp.float32
+        ).astype(jnp.bfloat16)
+
+        @pl.when(jnp.logical_and(at > z, z == 0))
+        def _():
+            climb(at, above).start()
+
+        @pl.when(jnp.logical_and(at < z, z == top))
+        def _():
+            descend(at, below).start()
+
+        return carry
+
+    lax.fori_loop(0, tp_count, project, 0)
+
+    def add_to(at, arrived):
+        parts[at] = (
+            parts[at].astype(jnp.float32) + arrived[at].astype(jnp.float32)
+        ).astype(jnp.bfloat16)
+
+    def hand_on(step, carry):
+        at = near_first(z, top - step, tp_count)
+
+        @pl.when(jnp.logical_and(at > z, z > 0))
+        def _():
+            climb(at, above).wait_recv()
+            add_to(at, from_below)
+            climb(at, above).start()
+
+        @pl.when(jnp.logical_and(at < z, z < top))
+        def _():
+            descend(at, below).wait_recv()
+            add_to(at, from_above)
+            descend(at, below).start()
+
+        return carry
+
+    lax.fori_loop(0, top, hand_on, 0)
+    stream_ref[...] = residual_ref[...].astype(jnp.float32) + parts[z].astype(jnp.float32)
+
+    @pl.when(z > 0)
+    def _():
+        climb(z, above).wait_recv()
+        stream_ref[...] += from_below[z].astype(jnp.float32)
+
+    @pl.when(z < top)
+    def _():
+        descend(z, below).wait_recv()
+        stream_ref[...] += from_above[z].astype(jnp.float32)
+
+    stream = stream_ref[...]
+    normed_ref[...] = (
+        stream
+        * lax.rsqrt(jnp.mean(stream * stream, axis=-1, keepdims=True) + 1e-06)
+        * gain_ref[...].astype(jnp.float32)
+    ).astype(jnp.bfloat16)
+
+    for step in range(1, tp_count):
+        peer = lax.rem(z + step, tp_count)
+        for copy in gives(peer, z):
+            copy.wait_send()
+
+    def drain(at, carry):
+        pl.when(at > z)(climb(at, above).wait_send)
+        pl.when(at < z)(descend(at, below).wait_send)
+        return carry
+
+    lax.fori_loop(0, tp_count, drain, 0)
+
+
+def attend_rows(
+    queries, new_keys, new_values, cache_keys, cache_values, out_weight, residual, norm_gain
+):
+    tp_count = lax.axis_size("tp")
+    group_rows, head_columns = queries.shape
+    own_rows, width = residual.shape
+    key_rows = cache_keys.shape[1] * tp_count + group_rows
+    dma = pltpu.SemaphoreType.DMA
+    block = (own_rows, width)
+    in_vmem = pl.BlockSpec(memory_space=pltpu.VMEM)
+    in_any = pl.BlockSpec(memory_space=pl.ANY)
+    return pl.pallas_call(
+        functools.partial(attend_kernel, tp_count),
+        out_shape=(
+            jax.ShapeDtypeStruct(block, jnp.float32),
+            jax.ShapeDtypeStruct(block, jnp.bfloat16),
+        ),
+        in_specs=[in_vmem] + [in_any] * 5 + [in_vmem] * 2,
+        out_specs=(in_vmem, in_vmem),
+        scratch_shapes=[
+            pltpu.VMEM((key_rows, HD), jnp.bfloat16),
+            pltpu.VMEM((key_rows, HD), jnp.bfloat16),
+            pltpu.VMEM((head_columns, width), jnp.bfloat16),
+            pltpu.VMEM((own_rows, head_columns), jnp.bfloat16),
+            pltpu.VMEM((tp_count,) + block, jnp.bfloat16),
+            pltpu.VMEM((tp_count,) + block, jnp.bfloat16),
+            pltpu.VMEM((tp_count,) + block, jnp.bfloat16),
+            dma((5,)),
+        ]
+        + [dma((tp_count,))] * 7,
+        compiler_params=pltpu.CompilerParams(
+            collective_id=1, has_side_effects=True, vmem_limit_bytes=48 * 2**20
+        ),
+        cost_estimate=pl.CostEstimate(
+            flops=4 * group_rows * key_rows * head_columns + 2 * group_rows * head_columns * width,
+            bytes_accessed=2 * head_columns * width,
+            transcendentals=0,
+        ),
+        name="attend_rows",
+    )(
+        queries,
+        new_keys,
+        new_values,
+        cache_keys,
+        cache_values,
+        out_weight,
+        residual,
+        norm_gain.reshape(1, width),
+    )
 
 
 def experts_kernel(
@@ -58,7 +292,9 @@
     other_y, other_core = side + 2 - 4 * y, side + 1 - 2 * core
     far_core = other_y + 1 - 2 * core
     own_rows, width = own_ref.shape
+    spare = weight_ref.shape[1]
     inner = gate.shape[1]
+    me = lax.axis_index(("side", "tp"))
     loads = [
         pltpu.make_async_copy(source.at[0], target, load_sem.at[at])
         for at, (source, target) in enumerate(((gate_hbm, gate), (up_hbm, up), (down_hbm, down)))
@@ -150,7 +386,8 @@
             parts[at_side, at_z].astype(jnp.float32) + arrived[...].astype(jnp.float32)
         ).astype(jnp.bfloat16)
 
-    rows[side, z] = own_ref[...]
+    rows[side, z, :, :width] = own_ref[...]
+    rows[side, z, :, width:] = weight_ref[...]
     spread(z)
     for load in loads:
         load.wait()
@@ -173,7 +410,7 @@
 
         def hide(at, carry):
             columns = pl.ds(pl.multiple_of(at * block, block), block)
-            taken = rows[:, at_z].reshape(count, width)
+            taken = rows[:, at_z, :, :width].reshape(count, width)
             gate_sum = jnp.dot(taken, gate[:, columns], preferred_element_type=jnp.float32)
             upward = jnp.dot(taken, up[:, columns], preferred_element_type=jnp.float32)
             hidden[:, columns] = (gate_sum / (1.0 + jnp.exp(-gate_sum)) * upward).astype(
@@ -187,7 +424,10 @@
         def show(at, carry):
             columns = pl.ds(pl.multiple_of(at * out_block, out_block), out_block)
             out = jnp.dot(hidden[...], down[:, columns], preferred_element_type=jnp.float32)
-            scale = weight_ref[:, at_z].reshape(count, 1)
+            listed = rows[:, at_z, :, width:].reshape(count, spare).astype(jnp.float32)
+            lane = lax.broadcasted_iota(jnp.int32, (count, spare), 1)
+            mine = jnp.logical_or(lane == me, lane == me + side_count * tp_count)
+            scale = jnp.sum(jnp.where(mine, listed, 0.0), axis=1, keepdims=True)
             parts[:, at_z, :, columns] = (
                 (out * scale).astype(jnp.bfloat16).reshape(side_count, own_rows, out_block)
             )
@@ -245,7 +485,7 @@
     lax.fori_loop(0, tp_count, drain, 0)
 
 
-def exchange_experts(normed, own_weight, gate_weight, up_weight, down_weight):
+def exchange_experts(normed, listed, gate_weight, up_weight, down_weight):
     side_count, tp_count = lax.axis_size("side"), lax.axis_size("tp")
     own_rows, width = normed.shape
     inner = gate_weight.shape[2]
@@ -260,7 +500,7 @@
         + [pl.BlockSpec(memory_space=pl.ANY)] * 3,
         out_specs=pl.BlockSpec(memory_space=pltpu.VMEM),
         scratch_shapes=[
-            pltpu.VMEM((side_count, tp_count) + block, jnp.bfloat16),
+            pltpu.VMEM((side_count, tp_count, own_rows, width + listed.shape[1]), jnp.bfloat16),
             pltpu.VMEM((side_count, tp_count) + block, jnp.bfloat16),
             pltpu.VMEM((half, tp_count) + block, jnp.bfloat16),
             pltpu.VMEM((tp_count,) + block, jnp.bfloat16),
@@ -291,7 +531,7 @@
         name="experts_exchange",
     )(
         normed,
-        own_weight.reshape(side_count, tp_count, own_rows, 1),
+        listed,
         gate_weight,
         up_weight,
         down_weight,
@@ -305,11 +545,14 @@
     weights = weights / jnp.sum(weights, axis=1, keepdims=True)
     named = expert_ids[:, :, None] == jnp.arange(experts_all)[None, None, :]
     per_expert = jnp.sum(jnp.where(named, weights[:, :, None], 0.0), axis=1)
+    if lax.axis_size("side") == 4 and 2 * experts_all <= 128:
+        high = lax.reduce_precision(per_expert, 8, 7)
+        spare = jnp.zeros((stream.shape[0], 128 - 2 * experts_all), jnp.float32)
+        listed = jnp.concatenate([high, per_expert - high, spare], axis=1).astype(jnp.bfloat16)
+        return stream + exchange_experts(normed, listed, gate_weight, up_weight, down_weight)
     all_weights = lax.all_gather(per_expert, ("side", "tp"), axis=0, tiled=True)
     me = lax.axis_index(("side", "tp"))
     own_weight = lax.dynamic_slice_in_dim(all_weights, me, 1, axis=1)
-    if lax.axis_size("side") == 4:
-        return stream + exchange_experts(normed, own_weight, gate_weight, up_weight, down_weight)
     rows = lax.all_gather(normed, ("side", "tp"), axis=0, tiled=True)
     gate_sum = jnp.dot(rows, gate_weight[0], preferred_element_type=jnp.float32)
     upward = jnp.dot(rows, up_weight[0], preferred_element_type=jnp.float32)
@@ -318,6 +561,62 @@
     weighted = (expert_out * own_weight).astype(jnp.bfloat16)
     mixture = lax.psum_scatter(weighted, ("side", "tp"), scatter_dimension=0, tiled=True)
     return stream + mixture.astype(jnp.float32)
+
+
+def attend_plain(
+    queries, new_keys, new_values, cache_keys, cache_values, out_weight, residual, norm_gain
+):
+    group_rows = queries.shape[0]
+    local_heads = queries.shape[1] // HD
+    head_kv = (lax.axis_index("tp") * local_heads + jnp.arange(local_heads)) // (H // KV)
+    query_heads = queries.reshape(group_rows, local_heads, HD)
+    score_scale = 1.0 / math.sqrt(HD)
+    initial = (
+        jnp.full((local_heads, group_rows), -1e30, jnp.float32),
+        jnp.zeros((local_heads, group_rows), jnp.float32),
+        jnp.zeros((local_heads, group_rows, HD), jnp.float32),
+    )
+    cache_both = lax.all_gather(
+        jnp.concatenate([cache_keys[0], cache_values[0]], axis=1), "tp", axis=0, tiled=True
+    )
+    key_width = cache_keys.shape[2]
+    key_piece = pick_heads(cache_both[:, :key_width], head_kv)
+    value_piece = pick_heads(cache_both[:, key_width:], head_kv)
+    scores = (
+        jnp.einsum("rhd,nhd->hrn", query_heads, key_piece, preferred_element_type=jnp.float32)
+        * score_scale
+    )
+    state_now = softmax_update(initial, scores, value_piece)
+    own_keys = pick_heads(new_keys, head_kv)
+    own_values = pick_heads(new_values, head_kv)
+    scores = (
+        jnp.einsum("rhd,nhd->hrn", query_heads, own_keys, preferred_element_type=jnp.float32)
+        * score_scale
+    )
+    positions = jnp.arange(group_rows)
+    visible = positions[None, :] <= positions[:, None]
+    scores = jnp.where(visible[None], scores, -1e30)
+    running, totals, context = softmax_update(state_now, scores, own_values)
+    attended = (
+        (context / totals[..., None])
+        .transpose(1, 0, 2)
+        .reshape(group_rows, local_heads * HD)
+        .astype(jnp.bfloat16)
+    )
+    own_rows = residual.shape[0]
+    attn_out = lax.psum_scatter(
+        jnp.dot(attended, out_weight, preferred_element_type=jnp.float32).astype(jnp.bfloat16),
+        "tp",
+        scatter_dimension=0,
+        tiled=True,
+    ).astype(jnp.float32)
+    stream = residual.astype(jnp.float32) + attn_out
+    normed = (
+        stream
+        * lax.rsqrt(jnp.mean(stream * stream, axis=-1, keepdims=True) + 1e-06)
+        * norm_gain.astype(jnp.float32)
+    ).astype(jnp.bfloat16)
+    return stream, normed
 
 
 def local(
@@ -337,56 +636,11 @@
 ):
     tp_count = lax.axis_size("tp")
     side_count = lax.axis_size("side")
-    group_rows = queries.shape[0]
-    local_heads = queries.shape[1] // HD
-    head_kv = (lax.axis_index("tp") * local_heads + jnp.arange(local_heads)) // (H // KV)
-    query_heads = queries.reshape(group_rows, local_heads, HD)
-    score_scale = 1.0 / math.sqrt(HD)
-    initial = (
-        jnp.full((local_heads, group_rows), -1e30, jnp.float32),
-        jnp.zeros((local_heads, group_rows), jnp.float32),
-        jnp.zeros((local_heads, group_rows, HD), jnp.float32),
-    )
-    cache_both = lax.all_gather(
-        jnp.concatenate([cache_keys[0], cache_values[0]], axis=1), "tp", axis=0, tiled=True
-    )
-    key_width = cache_keys.shape[2]
-    key_piece = pick_heads(cache_both[:, :key_width], head_kv)
-    value_piece = pick_heads(cache_both[:, key_width:], head_kv)
-    scores = (
-        jnp.einsum("rhd,nhd->hrn", query_heads, key_piece, preferred_element_type=jnp.float32)
-        * score_scale
-    )
-    state_now = softmax_update(initial, scores, value_piece)
-    own_keys = pick_heads(new_keys, head_kv)
-    own_values = pick_heads(new_values, head_kv)
-    scores = (
-        jnp.einsum("rhd,nhd->hrn", query_heads, own_keys, preferred_element_type=jnp.float32)
-        * score_scale
-    )
-    positions = jnp.arange(group_rows)
-    visible = positions[None, :] <= positions[:, None]
-    scores = jnp.where(visible[None], scores, -1e30)
-    running, totals, context = softmax_update(state_now, scores, own_values)
-    attended = (
-        (context / totals[..., None])
-        .transpose(1, 0, 2)
-        .reshape(group_rows, local_heads * HD)
-        .astype(jnp.bfloat16)
-    )
     own_rows = residual.shape[0]
-    attn_out = lax.psum_scatter(
-        jnp.dot(attended, out_weight, preferred_element_type=jnp.float32).astype(jnp.bfloat16),
-        "tp",
-        scatter_dimension=0,
-        tiled=True,
-    ).astype(jnp.float32)
-    stream = residual.astype(jnp.float32) + attn_out
-    normed = (
-        stream
-        * lax.rsqrt(jnp.mean(stream * stream, axis=-1, keepdims=True) + 1e-06)
-        * norm_gain.astype(jnp.float32)
-    ).astype(jnp.bfloat16)
+    attend = attend_rows if tp_count == KV else attend_plain
+    stream, normed = attend(
+        queries, new_keys, new_values, cache_keys, cache_values, out_weight, residual, norm_gain
+    )
     experts_all = side_count * tp_count
     top_count = expert_ids.shape[1]
     copies = own_rows * top_count

time: 250 us -> 187 us (0.75)
  Pallas kernels: 122 us -> 173 us
  blocking collectives: 35.1 us -> 0 us
  waiting for transfers between devices: 30.1 us -> 0 us
  matrix products: 24.1 us -> 0 us
  between operations: 13.7 us -> 0.05 us
  other arithmetic: 12.3 us -> 5.13 us
  local copies, waits for them, and re-layouts: 12.3 us -> 8.04 us
    pallas_call x0 -> x1, Pallas kernels: none -> 51.4 us  [attend_rows(): pl.pallas_call(functools.partial(attend_kernel, tp_count), out_shape=(jax...]
    all_gather x1 -> x0, blocking collectives: 35.1 us -> none  [dense_experts(): all_weights = lax.all_gather(per_expert, ('side', 'tp'), axis=0, tiled=True)]
    dot_general x5 -> x0, matrix products: 24.1 us -> none  [the longest x2 10.9 us: softmax_update(): jnp.einsum('hrn,nhd->hrd', exponent.astype(jnp.bfloat16), values, preferr...]
    all_gather x1 -> x0, waiting for transfers between devices: 22.4 us -> none  [local(): lax.all_gather(jnp.concatenate([cache_keys[0], cache_values[0]], axis=1),...]
    reduce_scatter x1 -> x0, waiting for transfers between devices: 7.68 us -> none  [local(): lax.psum_scatter(jnp.dot(attended, out_weight, preferred_element_type=jnp...]
    reduce_sum x2 -> x0, other arithmetic: 6.95 us -> none  [the longest x1 5.66 us: softmax_update(): totals = totals * factor + jnp.sum(exponent, axis=-1)]
    gather x4 -> x0, local copies, waits for them, and re-layouts: 3.91 us -> none  [pick_heads(): return jnp.take(shaped, head_kv, axis=1)]
    unnamed x26 -> x14, local copies, waits for them, and re-layouts: 4.7 us -> 6.94 us
  transfers between devices with their start and end apart: 2 -> 0, of which waited for: 2 -> 0; matrix products, arithmetic and copies ran while one was open for 5% -> 0% of each run, Pallas kernels for 0% -> 0%
where the time goes in v3:
time: 187 us; the launch traced here: 186 us
  Pallas kernels  173 us (93%)
  local copies, waits for them, and re-layouts  8.04 us (4%)
  other arithmetic  5.13 us (3%)
    pallas_call x1, Pallas kernels, exchange_experts(): pl.pallas_call(functools.partial(experts_kernel, side_count, tp_count), o...  122 us
    pallas_call x1, Pallas kernels, attend_rows(): pl.pallas_call(functools.partial(attend_kernel, tp_count), out_shape=(jax...  51.4 us
    unnamed x14, local copies, waits for them, and re-layouts  6.94 us

profile of v3, /device:TPU:0, one launch (start us, length us, event | category | flops | bytes accessed | tf_op | source)
XLA Modules:
  0.0 186.2 jit_solution(10864162582908921603)
XLA Ops:
  0.0 0.7 convert_reduce_fusion
  0.7 0.1 pad.2.clone
  0.8 0.7 convert_divide_fusion
  1.5 0.7 select_reduce_fusion
  2.2 0.7 reshape.6.gain_ref
  2.9 0.1 copy.20
  3.0 0.1 copy.18
  3.1 0.1 copy.19
  3.2 0.7 maximum_maximum_fusion.weight_ref
  3.9 0.0 copy-start
  3.9 1.2 copy-done
  5.1 0.0 copy-start.1
  5.2 1.0 copy-done.1
  6.2 0.0 copy-start.2
  6.2 1.0 copy-done.2
  7.2 0.0 copy-start.3
  7.2 1.0 copy-done.3
  8.3 0.0 copy-start.4
  8.3 0.9 copy-done.4
  9.2 0.0 copy-start.5
  9.2 0.9 copy-done.5
  10.1 51.4 %attend_rows.1 = (f32[128,2048]{1,0:T(8,128)S(1)}, bf16[128,2048]{1,0:T(8,128)(2,1)S(1)}) custom-call(bf16[512,1024]{1,0:T(8,128)(2,1)S(1)} %copy-done, bf16[512,512]{1,0:T(8,128)(2,1)S(1)} %copy-done.1, bf16[512,512]{1,0:T(8,128)(2,1)S(1)} %copy-done.2, bf16[1,128,512]{2,1,0:T(8,128)(2,1)S(1)} %copy-done.4, bf16[1,128,512]{2,1,0:T(8,128)(2,1)S(1)} %copy-done.5, ...), custom_call_target="tpu_custom_call" | custom-call | flops 4294967296 | bytes 4194304 | tf_op jit(solution)/shard_map/attend_rows/pallas_call | solution.py:244
  61.5 0.0 copy-start.6
  61.5 0.8 copy-done.6
  62.3 121.5 %experts_exchange.1 = f32[128,2048]{1,0:T(8,128)} custom-call(bf16[128,2048]{1,0:T(8,128)(2,1)} %copy-done.6, bf16[128,128]{1,0:T(8,128)(2,1)} %maximum_maximum_fusion.weight_ref, bf16[1,2048,768]{2,1,0:T(8,128)(2,1)} %gate_hbm.1, bf16[1,2048,768]{2,1,0:T(8,128)(2,1)} %up_hbm.1, bf16[1,768,2048]{2,1,0:T(8,128)(2,1)} %down_hbm.1), custom_call_target="tpu_custom_call" | custom-call | flops 19327352832 | bytes 9437184 | tf_op jit(solution)/shard_map/experts_exchange/pallas_call | solution.py:496
  183.8 2.3 %add.3 = f32[128,2048]{1,0:T(8,128)} add(f32[128,2048]{1,0:T(8,128)S(1)} %get-tuple-element.7, f32[128,2048]{1,0:T(8,128)} %experts_exchange.1) | non-fusion elementwise | flops 262144 | bytes 3145728 | tf_op jit(solution)/shard_map/add | solution.py:552
  (3 shorter events, 0.0 us)
Async XLA Ops:
  3.9 1.2 copy-start
  5.1 1.0 copy-start.1
  6.2 1.0 copy-start.2
  7.2 1.0 copy-start.3
  8.3 0.9 copy-start.4
  9.2 0.9 copy-start.5
  61.5 0.8 copy-start.6

commit v4 on v3

--- a/solution.py
+++ b/solution.py
@@ -240,7 +240,7 @@
     dma = pltpu.SemaphoreType.DMA
     block = (own_rows, width)
     in_vmem = pl.BlockSpec(memory_space=pltpu.VMEM)
-    in_any = pl.BlockSpec(memory_space=pl.ANY)
+    in_any = pl.BlockSpec(memory_space=pltpu.HBM)
     return pl.pallas_call(
         functools.partial(attend_kernel, tp_count),
         out_shape=(
@@ -261,7 +261,7 @@
         ]
         + [dma((tp_count,))] * 7,
         compiler_params=pltpu.CompilerParams(
-            collective_id=1, has_side_effects=True, vmem_limit_bytes=48 * 2**20
+            collective_id=1, has_side_effects=True, vmem_limit_bytes=58 * 2**20
         ),
         cost_estimate=pl.CostEstimate(
             flops=4 * group_rows * key_rows * head_columns + 2 * group_rows * head_columns * width,
@@ -389,15 +389,35 @@
     rows[side, z, :, :width] = own_ref[...]
     rows[side, z, :, width:] = weight_ref[...]
     spread(z)
+    inside = jnp.logical_and(z > 0, z < tp_count - 1)
+
+    @pl.when(inside)
+    def _():
+        next_z = near_first(z, 1, tp_count)
+        wait_row(side, next_z)
+        spread(next_z)
+
     for load in loads:
         load.wait()
 
+    def back_y(at_z):
+        to_core(1 - y, at_z).wait_recv()
+        add_to_part(other_y, at_z, from_core.at[1 - y, at_z])
+        to_y(at_z).start()
+        to_core(y, at_z).wait_recv()
+        add_to_part(side, at_z, from_core.at[y, at_z])
+
+    def return_order(step):
+        turn = jnp.where(step == 0, tp_count - 2, tp_count - 1 - step)
+        return near_first(z, jnp.where(step == 1, tp_count - 1, turn), tp_count)
+
     def forward(step, carry):
         at_z = near_first(z, step, tp_count)
-
-        @pl.when(step + 1 < tp_count)
+        ahead = step + jnp.where(inside, 2, 1)
+
+        @pl.when(ahead < tp_count)
         def _():
-            next_z = near_first(z, step + 1, tp_count)
+            next_z = near_first(z, ahead, tp_count)
             wait_row(side, next_z)
             spread(next_z)
 
@@ -405,6 +425,11 @@
         pass_on(at_z).start()
         wait_row(other_core, at_z)
         wait_row(far_core, at_z)
+
+        @pl.when(step == tp_count - 1)
+        def _():
+            back_y(return_order(0))
+
         count = side_count * own_rows
         block = piece(inner, 256)
 
@@ -440,19 +465,14 @@
 
     lax.fori_loop(0, tp_count, forward, 0)
 
-    def back_y(step, carry):
-        at_z = near_first(z, tp_count - 1 - step, tp_count)
-        to_core(1 - y, at_z).wait_recv()
-        add_to_part(other_y, at_z, from_core.at[1 - y, at_z])
-        to_y(at_z).start()
-        to_core(y, at_z).wait_recv()
-        add_to_part(side, at_z, from_core.at[y, at_z])
+    def next_y(step, carry):
+        back_y(return_order(step))
         return carry
 
-    lax.fori_loop(0, tp_count, back_y, 0)
+    lax.fori_loop(1, tp_count, next_y, 0)
 
     def back_z(step, carry):
-        at_z = near_first(z, tp_count - 1 - step, tp_count)
+        at_z = return_order(step)
         to_y(at_z).wait_recv()
         add_to_part(side, at_z, from_y.at[at_z])
         to_line(at_z, z, at_z).start()

time: 187 us -> 177 us (0.947)
  local copies, waits for them, and re-layouts: 8.04 us -> 1.69 us
  Pallas kernels: 173 us -> 170 us
    unnamed x14 -> x2, local copies, waits for them, and re-layouts: 6.94 us -> 0.01 us
    pallas_call x1, Pallas kernels: 122 us -> 116 us  [exchange_experts(): pl.pallas_call(functools.partial(experts_kernel, side_count, tp_count), o...]
    pallas_call x1, Pallas kernels: 51.4 us -> 54.1 us  [attend_rows(): pl.pallas_call(functools.partial(attend_kernel, tp_count), out_shape=(jax...]
where the time goes in v4:
time: 177 us
  Pallas kernels  170 us (96%)
  other arithmetic  5.14 us (3%)
    pallas_call x1, Pallas kernels, exchange_experts(): pl.pallas_call(functools.partial(experts_kernel, side_count, tp_count), o...  116 us
    pallas_call x1, Pallas kernels, attend_rows(): pl.pallas_call(functools.partial(attend_kernel, tp_count), out_shape=(jax...  54.1 us

profile of v4, /device:TPU:0, one launch (start us, length us, event | category | flops | bytes accessed | tf_op | source)
XLA Modules:
  0.0 177.1 jit_solution(8109082110855333546)
XLA Ops:
  0.0 0.7 convert_reduce_fusion
  0.7 0.1 pad.2.clone
  0.8 0.7 convert_divide_fusion
  1.5 0.7 select_reduce_fusion
  2.2 1.3 reshape.6.gain_ref
  3.5 0.1 copy.20
  3.6 0.1 copy.18
  3.7 0.1 copy.19
  3.8 0.7 maximum_maximum_fusion.weight_ref
  4.5 54.1 %attend_rows.1 = (f32[128,2048]{1,0:T(8,128)}, bf16[128,2048]{1,0:T(8,128)(2,1)}) custom-call(bf16[512,1024]{1,0:T(8,128)(2,1)} %q_ref.1, bf16[512,512]{1,0:T(8,128)(2,1)} %new_k.1, bf16[512,512]{1,0:T(8,128)(2,1)} %new_v.1, bf16[1,128,512]{2,1,0:T(8,128)(2,1)} %cache_k.1, bf16[1,128,512]{2,1,0:T(8,128)(2,1)} %cache_v.1, bf16[1024,2048]{1,0:T(8,128)(2,1)} %out_hbm.1, ...), custom_call_target="tpu_custom_call" | custom-call | flops 4294967296 | bytes 4194304 | tf_op jit(solution)/shard_map/attend_rows/pallas_call | solution.py:244
  58.6 0.0 copy-start
  58.6 116.1 %experts_exchange.1 = f32[128,2048]{1,0:T(8,128)} custom-call(bf16[128,2048]{1,0:T(8,128)(2,1)} %get-tuple-element.8.own_ref, bf16[128,128]{1,0:T(8,128)(2,1)} %maximum_maximum_fusion.weight_ref, bf16[1,2048,768]{2,1,0:T(8,128)(2,1)} %gate_hbm.1, bf16[1,2048,768]{2,1,0:T(8,128)(2,1)} %up_hbm.1, bf16[1,768,2048]{2,1,0:T(8,128)(2,1)} %down_hbm.1), custom_call_target="tpu_custom_call" | custom-call | flops 19327352832 | bytes 9437184 | tf_op jit(solution)/shard_map/experts_exchange/pallas_call | solution.py:516
  174.8 0.0 copy-done
  174.8 2.3 %add.3 = f32[128,2048]{1,0:T(8,128)} add(f32[128,2048]{1,0:T(8,128)S(1)} %copy-done, f32[128,2048]{1,0:T(8,128)} %experts_exchange.1) | non-fusion elementwise | flops 262144 | bytes 3145728 | tf_op jit(solution)/shard_map/add | solution.py:572
  (3 shorter events, 0.0 us)
Async XLA Ops:
  58.6 116.1 %copy-start = (f32[128,2048]{1,0:T(8,128)S(1)}, f32[128,2048]{1,0:T(8,128)}, u32[]{:S(2)}) copy-start(f32[128,2048]{1,0:T(8,128)} %get-tuple-element.7) | copy-start | bytes 3145732
